TPU v7x, 512 devices: a whole 4x8x8 slice. The times are simulated.
512 devices in a mesh: loop: 32 (over x_hi, y, core), orb: 16 (over z, x_lo).
Axes of the slice: x: 4 (x_hi: 2, x_lo: 2; x = x_hi * 2 + x_lo), y: 8, z: 8, core: 2. Of those that a mesh axis runs over, the one named last changes fastest.
Arguments:
- cholesky: bfloat16 [4096, 65536], P('loop', 'orb'), may hold values from -0.0234375 to 0.0234375
- green_half: bfloat16 [1536, 65536], P('loop', 'orb'), may hold values from -6 to 6
- partners: int32 [256, 2], replicated, may hold values from 0 to 1535, as said below
Outputs:
- green_copied: bfloat16 [1536, 65536], P('loop', 'orb')
- force_bias: float32 [1536, 4096], P('orb', 'loop')
Inputs may be any that keep to these rules, and one draw needn't show every extreme that they name: `partners`: column 0 is a source walker, column 1 a destination walker. Destinations are distinct, sources are distinct, and no source is a destination. Each block of 48 consecutive walkers holds exactly 8 destinations and exactly 8 sources.
All inputs are finite; a program needn't handle non-finite values.
Results may differ from a plain program's by a relative error of at most 0.001.
Values may be sent and summed in bfloat16 or wider, within the bound.
A program may use at most 64 MiB of HBM per device.

v0:
```python
import jax
import jax.numpy as jnp
from jax import lax
from jax.sharding import PartitionSpec as P


def contract(shard_rows, cholesky):
    return lax.dot_general(
        shard_rows, cholesky, (((1,), (1,)), ((), ())), preferred_element_type=jnp.float32
    )


def local(cholesky, green_half, partners):
    loop_count = lax.axis_size("loop")
    block_rows = green_half.shape[0]
    walkers = block_rows * loop_count
    events = partners.shape[0]
    per_block = events // loop_count
    sources = partners[:, 0]
    targets = partners[:, 1]
    first_row = lax.axis_index("loop") * block_rows
    walker_index = jnp.arange(walkers, dtype=jnp.int32)
    event_index = jnp.arange(events, dtype=jnp.int32)
    target_hits = targets[None, :] == walker_index[:, None]
    overwritten = jnp.any(target_hits, axis=1)
    anchor = jnp.where(
        overwritten, jnp.sum(jnp.where(target_hits, sources[None, :], 0), axis=1), walker_index
    )
    local_flags = lax.dynamic_slice_in_dim(overwritten, first_row, block_rows)
    local_targets = jnp.nonzero(local_flags, size=per_block)[0].astype(jnp.int32)
    compact_rows = walker_index.shape[0]
    vector_count = cholesky.shape[0]
    initial = (
        jnp.zeros((compact_rows, vector_count), jnp.float32),
        jnp.zeros((per_block, green_half.shape[1]), jnp.float32),
    )
    partial_value = contract(lax.all_gather(green_half, "loop", axis=0, tiled=True), cholesky)
    compact_bias = partial_value
    picked = initial[1]
    compact_bias, picked = (compact_bias, picked)
    owner_block = sources // block_rows
    earlier = event_index[None, :] < event_index[:, None]
    slot_rank = jnp.sum(
        jnp.logical_and(earlier, owner_block[None, :] == owner_block[:, None]).astype(jnp.int32),
        axis=1,
    )
    own_events = jnp.nonzero(owner_block == lax.axis_index("loop"), size=per_block)[0].astype(
        jnp.int32
    )
    packed = jnp.take(green_half, jnp.take(sources, own_events) - first_row, axis=0)
    arrived = lax.all_gather(packed, "loop", axis=0, tiled=True)
    event_of = jnp.sum(jnp.where(target_hits, event_index[None, :], 0), axis=1)
    local_events = jnp.take(event_of, first_row + local_targets)
    copied = jnp.take(arrived, jnp.take(owner_block * per_block + slot_rank, local_events), axis=0)
    new_green = green_half.at[local_targets].set(copied)
    full_bias = jnp.take(compact_bias, jnp.take(walker_index, anchor), axis=0)
    bias_share = lax.psum_scatter(full_bias, "orb", scatter_dimension=0, tiled=True)
    return (new_green, bias_share)


def solution(mesh):
    return jax.shard_map(
        local,
        mesh=mesh,
        in_specs=(P("loop", "orb"), P("loop", "orb"), P()),
        out_specs=(P("loop", "orb"), P("orb", "loop")),
        check_vma=False,
    )
```

profile of v0, /device:TPU:24, one launch (start us, length us, event | category | flops | bytes accessed | tf_op | source)
XLA Modules:
  0.0 306.0 jit_solution(8178744544804263753)
XLA Ops:
  7.2 0.0 copy-start
  7.2 0.0 all-gather.5.cloned.1.call-start
  7.2 1.8 copy.10
  9.1 0.0 all-gather.5.cloned.1.call-update
  9.1 0.0 all-gather.3.cloned.1.call-start
  9.2 0.7 fusion.20
  9.9 0.8 add_select_fusion
  10.6 0.3 reduce-window.27
  11.0 0.1 slice.15
  11.1 0.1 slice_reduce_fusion
  11.2 0.1 broadcast_add_fusion
  11.3 2.3 scatter_custom_fusion.1
  13.6 0.2 reduce-window.29
  13.8 0.6 fusion.8
  14.4 0.7 compare_select_fusion.6
  15.1 0.6 gather_fusion.5
  15.7 0.7 compare_and_fusion.2
  16.4 1.7 gather_fusion.1
  18.1 0.7 broadcast_select_fusion.1
  18.8 0.0 all-gather.3.cloned.1.call-update
  18.8 0.0 reduce-scatter.2.cloned.1.call-start
  18.9 0.3 fusion
  19.2 0.8 fusion.17
  20.0 0.1 fusion.16
  20.0 0.1 copy.7
  20.1 0.1 reduce-window.26
  20.2 0.1 fusion.6
  20.3 0.9 scatter_custom_fusion
  21.2 0.2 select_n.234
  21.4 0.6 select_reduce_fusion
  22.0 8.4 %gather_fusion.2 = s32[1536]{0:T(1024)S(1)} fusion(s32[1536]{0:T(1024)S(1)} %iota.34, s32[2048]{0:T(1024)S(1)} %pad_clamp_fusion.1), kind=kCustom, calls=%fused_computation.5 | custom fusion | bytes 18432 | tf_op jit(solution)/shard_map/jit(_take)/gather | solution.py:56
  30.5 107.9 %all-gather.5.cloned.1.call-done = bf16[1536,4096]{1,0:T(8,128)(2,1)} async-done(((bf16[48,4096]{1,0:T(8,128)(2,1)}), bf16[1536,4096]{1,0:T(8,128)(2,1)}) %all-gather.5.cloned.1.call-update) | async-done | bytes 12582928 | tf_op jit(solution)/shard_map/all_gather | solution.py:37
  138.4 0.0 copy-done
  138.4 6.4 %fusion.21 = f32[1536,128]{1,0:T(8,128)S(1)} fusion(bf16[1536,4096]{1,0:T(8,128)(2,1)} %all-gather.5.cloned.1.call-done, bf16[128,4096]{1,0:T(8,128)(2,1)S(1)} %copy-done), kind=kOutput, calls=%fused_computation.85 | convolution fusion | flops 1610612736 | bytes 14417920 | tf_op jit(solution)/shard_map/dot_general | solution.py:8
  144.9 2.6 gather_fusion.3
  147.5 0.0 copy-start.1
  147.5 1.1 broadcast_select_fusion
  148.6 0.0 reduce-scatter.2.cloned.1.call-update
  148.6 0.7 fusion.11
  149.4 0.6 gather_fusion
  150.0 0.7 compare_select_fusion.7
  150.7 0.2 convert_reduce_fusion
  150.9 0.6 gather_fusion.4
  151.6 72.8 %all-gather.3.cloned.1.call-done = bf16[256,4096]{1,0:T(8,128)(2,1)} async-done(((bf16[8,4096]{1,0:T(8,128)(2,1)}), bf16[256,4096]{1,0:T(8,128)(2,1)}) %all-gather.3.cloned.1.call-update) | async-done | bytes 2097168 | tf_op jit(solution)/shard_map/all_gather | solution.py:51
  224.4 0.0 copy-done.1
  224.4 1.9 scatter_custom_fusion.2
  226.4 0.0 copy-start.2
  226.4 73.1 %reduce-scatter.2.cloned.1.call-done = f32[96,128]{1,0:T(8,128)} async-done(((f32[1536,128]{1,0:T(8,128)}), f32[96,128]{1,0:T(8,128)}) %reduce-scatter.2.cloned.1.call-update) | async-done | bytes 49168 | tf_op jit(solution)/shard_map/reduce_scatter | solution.py:57
  299.5 0.0 copy-done.2
  (19 shorter events, 0.2 us)
Async XLA Ops:
  7.2 131.3 %copy-start = (bf16[128,4096]{1,0:T(8,128)(2,1)S(1)}, bf16[128,4096]{1,0:T(8,128)(2,1)}, u32[]{:S(2)}) copy-start(bf16[128,4096]{1,0:T(8,128)(2,1)} %param.5) | copy-start | bytes 3145732
  7.2 131.3 %all-gather.5.cloned.1.call-start = ((), (), s32[]{:S(2)}) async-start(), calls=%async_computation.2 | async-start | bytes 12976128 | tf_op jit(solution)/shard_map/all_gather | solution.py:37
  9.1 215.3 %all-gather.3.cloned.1.call-start = ((), (), s32[]{:S(2)}) async-start(), calls=%async_computation.1 | async-start | bytes 2162688 | tf_op jit(solution)/shard_map/all_gather | solution.py:51
  18.8 280.7 %reduce-scatter.2.cloned.1.call-start = ((), (), s32[]{:S(2)}) async-start(), calls=%async_computation.3 | async-start | bytes 835584 | tf_op jit(solution)/shard_map/reduce_scatter | solution.py:57
  147.5 77.0 %copy-start.1 = (bf16[48,4096]{1,0:T(8,128)(2,1)S(1)}, bf16[48,4096]{1,0:T(8,128)(2,1)}, u32[]{:S(2)}) copy-start(bf16[48,4096]{1,0:T(8,128)(2,1)} %copy.10) | copy-start | bytes 1179652
  226.4 73.1 %copy-start.2 = (bf16[48,4096]{1,0:T(8,128)(2,1)}, bf16[48,4096]{1,0:T(8,128)(2,1)S(1)}, u32[]{:S(2)}) copy-start(bf16[48,4096]{1,0:T(8,128)(2,1)S(1)} %scatter_custom_fusion.2) | copy-start | bytes 1179652
Sparse Core Ops, SparseCore 0:
  11.9 126.4 all-gather.4
  141.8 82.5 all-gather.2
  227.8 71.6 reduce-scatter.1
where the time goes:
time: 306 us
  waiting for transfers between devices  254 us (83%)
  local copies, waits for them, and re-layouts  16.8 us (5%)
  other arithmetic  14.9 us (5%)
  between operations  14 us (5%)
  matrix products  6.41 us (2%)
    all_gather x1, waiting for transfers between devices, local(): lax.all_gather(green_half, 'loop', axis=0, tiled=True)  108 us
    reduce_scatter x1, waiting for transfers between devices, local(): lax.psum_scatter(full_bias, 'orb', scatter_dimension=0, tiled=True)  73.1 us
    all_gather x1, waiting for transfers between devices, local(): arrived = lax.all_gather(packed, 'loop', axis=0, tiled=True)  72.8 us
    gather x2, local copies, waits for them, and re-layouts, local(): full_bias = jnp.take(compact_bias, jnp.take(walker_index, anchor), axis=0)  11 us
    dot_general x1, matrix products, contract(): lax.dot_general(shard_rows, cholesky, (((1,), (1,)), ((), ())), preferred...  6.41 us
  transfers between devices with their start and end apart: 3, of which 3 were waited for; matrix products, arithmetic and copies ran while one was open for 12% of the time, Pallas kernels for 0%

commit v1 on v0

v1 whole, which is shorter than its diff:
```python
import jax
import jax.numpy as jnp
from jax import lax
from jax.experimental import pallas as pl
from jax.experimental.pallas import tpu as pltpu
from jax.sharding import PartitionSpec as P

MESH = pl.DeviceIdType.MESH
NY, NZ, NX = 8, 8, 4
F32, BF16 = jnp.float32, jnp.bfloat16


def dot_t(a, b):
    return lax.dot_general(a, b, (((1,), (1,)), ((), ())), preferred_element_type=F32)


def split3(v):
    hi = v.astype(BF16)
    rest = v - hi.astype(F32)
    mid = rest.astype(BF16)
    lo = (rest - mid.astype(F32)).astype(BF16)
    return hi, mid, lo


def pick_rows(onehot, v):
    hi, mid, lo = split3(v)
    return (
        jnp.dot(onehot, hi, preferred_element_type=F32)
        + jnp.dot(onehot, mid, preferred_element_type=F32)
    ) + jnp.dot(onehot, lo, preferred_element_type=F32)


def iota(shape, dim):
    return lax.broadcasted_iota(jnp.int32, shape, dim).astype(F32)


def kernel(
    chol, green, prow, new_green, bias,
    gb, w, cs, rx, zs, rz, fix, fx, rfx, fzs, rfz, s_acc, s_out, s_in, csrc, ch_out,
    y_ss, y_rs, b_ss, b_rs, p_ss, p_rs, x_ss, x_rs, z_ss, z_rs, fx_ss, fx_rs, fz_ss, fz_rs,
):
    rows = green.shape[0]
    half = green.shape[1] // 2
    vec = chol.shape[0]
    two = 2 * rows
    loop, orb = lax.axis_index("loop"), lax.axis_index("orb")
    h, y, c = lax.div(loop, 16), lax.rem(lax.div(loop, 2), NY), lax.rem(loop, 2)
    z, xl = lax.div(orb, 2), lax.rem(orb, 2)
    x = 2 * h + xl
    other = 1 - h

    def dev(dx=0, dy=0, dz=0, dc=0):
        xx = lax.rem(x + dx, NX)
        yy = lax.rem(y + dy + NY, NY)
        zz = lax.rem(z + dz, NZ)
        cc = lax.rem(c + dc, 2)
        return (lax.div(xx, 2) * 16 + yy * 2 + cc, zz * 2 + lax.rem(xx, 2))

    def remote(src, dst, ss, rs, to):
        return pltpu.make_async_remote_copy(
            src_ref=src, dst_ref=dst, send_sem=ss, recv_sem=rs, device_id=to, device_id_type=MESH
        )

    barrier = pltpu.get_barrier_semaphore()
    peers = [dev(dy=1), dev(dy=-1), dev(dc=1)]
    peers += [dev(dx=k) for k in range(1, NX)] + [dev(dz=k) for k in range(1, NZ)]
    for peer in peers:
        pl.semaphore_signal(barrier, inc=1, device_id=peer, device_id_type=MESH)

    own_cols = pl.ds(pl.multiple_of(h * half, half), half)
    far_cols = pl.ds(pl.multiple_of(other * half, half), half)
    gb[0, 0, c] = green[:, own_cols]
    s_out[0:rows] = green[:, far_cols]
    ch_out[...] = chol[:, far_cols]
    w[pl.ds(pl.multiple_of(h * vec, vec), vec)] = chol[:, own_cols]
    pl.semaphore_wait(barrier, len(peers))

    def y_copy(pq, d, step):
        return remote(
            gb.at[pq, d % NY, c], gb.at[pq, (d - step) % NY, c],
            y_ss.at[pq, 0 if step > 0 else 1, abs(d)], y_rs.at[pq, (d - step) % NY], dev(dy=step),
        )

    def b_copy(pq, d):
        return remote(
            gb.at[pq, d % NY, c], gb.at[pq, d % NY, c], b_ss.at[pq, d % NY], b_rs.at[pq, d % NY], dev(dc=1)
        )

    def b_wait(pq, d):
        remote(
            gb.at[pq, d % NY, 1 - c], gb.at[pq, d % NY, 1 - c], b_ss.at[pq, d % NY], b_rs.at[pq, d % NY], dev(dc=1)
        ).wait_recv()

    q_copy = remote(s_out.at[pl.ds(0, rows)], gb.at[1, 0, c], p_ss.at[0], p_rs.at[0], dev(dx=2))
    h_copy = remote(
        ch_out, w.at[pl.ds(pl.multiple_of(h * vec, vec), vec)], p_ss.at[1], p_rs.at[1], dev(dx=2)
    )
    h_in = remote(
        ch_out, w.at[pl.ds(pl.multiple_of(other * vec, vec), vec)], p_ss.at[1], p_rs.at[1], dev(dx=2)
    )
    started = []

    def go(copy):
        copy.start()
        started.append(copy)

    go(y_copy(0, 0, 1))
    go(y_copy(0, 0, -1))
    q_copy.start()
    go(b_copy(0, 0))

    events = prow.shape[1]
    src_row, tgt_row = prow[0:1, :].astype(F32), prow[1:2, :].astype(F32)
    diag = iota((events, events), 0) == iota((events, events), 1)
    tgt_col = jnp.sum(jnp.where(diag, tgt_row, 0.0), axis=1, keepdims=True)
    pos_row = jnp.sum(jnp.where(tgt_col < tgt_row, 1.0, 0.0), axis=0, keepdims=True)
    placed = iota((events, events), 0) == pos_row
    src_col = jnp.sum(jnp.where(placed, src_row, 0.0), axis=1, keepdims=True)
    csrc[...] = jnp.broadcast_to(src_col, csrc.shape)
    per = 8
    fix[...] = jnp.zeros_like(fix)
    s_acc[...] = jnp.zeros_like(s_acc)
    own_block = loop
    far_block = other * 16 + lax.rem(loop, 16)
    s_src = jnp.concatenate(
        [
            csrc[pl.ds(pl.multiple_of(own_block * per, per), per), :],
            csrc[pl.ds(pl.multiple_of(far_block * per, per), per), :],
        ],
        axis=0,
    )

    q_copy.wait_recv()
    go(y_copy(1, 0, 1))
    go(y_copy(1, 0, -1))
    go(b_copy(1, 0))
    q_copy.wait_send()
    go(h_copy)

    parity_here = lax.rem(y + xl, 2)

    def place(pq, d):
        hb = h if pq == 0 else other
        yb = lax.rem(y + (d % NY), NY)
        return hb, yb, 4 * hb + lax.div(yb, 2)

    def x_copy(pq, d, dx, slot):
        to = lax.div(lax.rem(x + dx, NX), 2)
        return remote(
            cs.at[pq, d % NY, to], rx.at[dx - 1, slot], x_ss.at[dx - 1, slot], x_rs.at[dx - 1, slot], dev(dx=dx)
        )

    def compute(pq, d):
        b_wait(pq, d)
        hb, yb, slot = place(pq, d)
        a = gb[pq, d % NY].reshape(two, half)
        part = dot_t(a, w[...])
        cs[pq, d % NY, 0] = part[:, :vec]
        cs[pq, d % NY, 1] = part[:, vec:]

        @pl.when(parity_here == d % 2)
        def _():
            x_copy(pq, d, 2, slot).start()

        @pl.when(parity_here != d % 2)
        def _():
            x_copy(pq, d, 1, slot).start()
            x_copy(pq, d, 3, slot).start()

        base = ((8 * hb + yb) * two).astype(F32)
        lane = iota((events, two), 1)
        oh = jnp.where(csrc[:, :two] - base == lane, 1.0, 0.0).astype(BF16)
        fix[...] += pick_rows(oh, part)
        oh_s = jnp.where(s_src[:, :two] - base == lane[:16], 1.0, 0.0).astype(BF16)
        s_acc[...] += jnp.dot(oh_s, a, preferred_element_type=F32)

    def z_stage(pq, d):
        _, _, slot = place(pq, d)

        @pl.when(parity_here == d % 2)
        def _():
            for dx in range(1, NX):
                x_copy(pq, d, dx, slot).wait_recv()
            zs[slot] = (cs[pq, d % NY, h] + rx[0, slot]) + (rx[1, slot] + rx[2, slot])
            k = lax.rem(slot - z + NZ, NZ)

            @pl.when(k != 0)
            def _():
                remote(zs.at[slot], rz.at[k], z_ss.at[k], z_rs.at[k], dev(dz=k)).start()

    def arrive(pq, d):
        remote(gb.at[pq, d % NY, c], gb.at[pq, d % NY, c], y_ss.at[pq, 0, 0], y_rs.at[pq, d % NY], dev(dy=1)).wait_recv()

    def take(pq, d):
        arrive(pq, d)
        up_end, down_end = (4, 3) if pq == 0 else (3, 4)
        if d < 0 and -d < up_end:
            go(y_copy(pq, d, 1))
        if 0 < d < down_end:
            go(y_copy(pq, d, -1))
        go(b_copy(pq, d))

    take(0, -1)
    take(0, 1)
    take(1, -1)
    take(1, 1)
    take(0, -2)
    take(0, 2)
    h_in.wait_recv()
    compute(0, 0)
    compute(1, 0)
    take(1, -2)
    take(1, 2)
    for d in (-1, 1):
        compute(0, d)
        compute(1, d)
    take(0, -3)
    take(0, 3)
    z_stage(0, 0)
    z_stage(1, 0)
    compute(0, -2)
    compute(0, 2)
    take(1, -3)
    take(1, 3)
    compute(1, -2)
    compute(1, 2)
    for d in (-1, 1):
        z_stage(0, d)
        z_stage(1, d)
    compute(0, -3)
    compute(0, 3)
    take(0, -4)
    take(1, 4)
    for d in (-2, 2):
        z_stage(0, d)
        z_stage(1, d)
    compute(1, -3)
    compute(1, 3)
    compute(0, 4)
    compute(1, 4)

    full = fix[...]
    for zz in range(NZ):
        for par in range(2):
            r0 = (2 * zz + par) * 16
            fx[par, 0, zz] = full[r0 : r0 + 16, :vec]
            fx[par, 1, zz] = full[r0 : r0 + 16, vec:]

    def fx_copy(dx):
        xx = lax.rem(x + dx, NX)
        return remote(fx.at[lax.rem(xx, 2), lax.div(xx, 2)], rfx.at[dx - 1], fx_ss.at[dx - 1], fx_rs.at[dx - 1], dev(dx=dx))

    for dx in range(1, NX):
        go(fx_copy(dx))
    s_out[0:16] = s_acc[...].astype(BF16)
    s_copy = remote(s_out.at[pl.ds(0, 16)], s_in, p_ss.at[2], p_rs.at[2], dev(dx=2))
    go(s_copy)
    for d in (-3, 3):
        z_stage(0, d)
        z_stage(1, d)
    z_stage(0, 4)
    z_stage(1, 4)
    for dx in range(1, NX):
        fx_copy(dx).wait_recv()
    fzs[...] = (fx[xl, h] + rfx[0]) + (rfx[1] + rfx[2])

    def fz_copy(k):
        return remote(fzs.at[lax.rem(z + k, NZ)], rfz.at[k], fz_ss.at[k], fz_rs.at[k], dev(dz=k))

    for k in range(1, NZ):
        go(fz_copy(k))

    s_copy.wait_recv()
    wide = (rows, events)
    first = (loop * rows).astype(F32)
    w_col = iota((rows, 1), 0) + first
    hit = jnp.sum(jnp.where(tgt_row == w_col, 1.0, 0.0), axis=1, keepdims=True)
    less = jnp.sum(jnp.where((tgt_row < w_col) & (tgt_row >= first), 1.0, 0.0), axis=1, keepdims=True)
    lane16 = iota((rows, 16), 1)
    put_own = jnp.where((hit > 0.5) & (less == lane16), 1.0, 0.0).astype(BF16)
    put_far = jnp.where((hit > 0.5) & (less + 8.0 == lane16), 1.0, 0.0).astype(BF16)
    keep = jnp.where((hit < 0.5) & (iota((rows, rows), 0) == iota((rows, rows), 1)), 1.0, 0.0).astype(BF16)
    new_green[:, own_cols] = (
        jnp.dot(keep, green[:, own_cols], preferred_element_type=F32)
        + jnp.dot(put_own, s_acc[...].astype(BF16), preferred_element_type=F32)
    ).astype(BF16)
    new_green[:, far_cols] = (
        jnp.dot(keep, green[:, far_cols], preferred_element_type=F32)
        + jnp.dot(put_far, s_in[...], preferred_element_type=F32)
    ).astype(BF16)

    o_first = (orb * two).astype(F32)
    o_col = iota((two, 1), 0)
    in_core = jnp.where(o_col >= rows, 1.0, 0.0)
    blk_first = o_first + in_core * rows
    o_abs = o_col + o_first
    o_hit = jnp.sum(jnp.where(tgt_row == o_abs, 1.0, 0.0), axis=1, keepdims=True)
    o_less = jnp.sum(jnp.where((tgt_row < o_abs) & (tgt_row >= blk_first), 1.0, 0.0), axis=1, keepdims=True)
    pick = jnp.where((o_hit > 0.5) & (o_less + in_core * 8.0 == iota((two, 16), 1)), 1.0, 0.0).astype(BF16)
    main = zs[z]
    tail = fzs[z]
    for k in range(1, NZ):
        remote(zs.at[0], rz.at[k], z_ss.at[k], z_rs.at[k], dev(dz=k)).wait_recv()
        main = main + rz[k]
    for k in range(1, NZ):
        fz_copy(k).wait_recv()
        tail = tail + rfz[k]
    bias[...] = jnp.where(o_hit > 0.5, pick_rows(pick, tail), main)

    for copy in started:
        copy.wait_send()
    for dx in range(1, NX):
        for slot in range(NZ):
            remote(cs.at[0, 0, 0], rx.at[dx - 1, slot], x_ss.at[dx - 1, slot], x_rs.at[dx - 1, slot], dev(dx=dx)).wait_send()
    for k in range(1, NZ):
        remote(zs.at[0], rz.at[k], z_ss.at[k], z_rs.at[k], dev(dz=k)).wait_send()


def local(cholesky, green_half, partners):
    rows, depth = green_half.shape
    vec = cholesky.shape[0]
    half, two = depth // 2, 2 * rows
    dma = pltpu.SemaphoreType.DMA
    vmem = pl.BlockSpec(memory_space=pltpu.VMEM)
    return pl.pallas_call(
        kernel,
        out_shape=(
            jax.ShapeDtypeStruct((rows, depth), BF16),
            jax.ShapeDtypeStruct((two, vec), F32),
        ),
        in_specs=[vmem] * 3,
        out_specs=(vmem, vmem),
        scratch_shapes=[
            pltpu.VMEM((2, NY, 2, rows, half), BF16),
            pltpu.VMEM((2 * vec, half), BF16),
            pltpu.VMEM((2, NY, 2, two, vec), F32),
            pltpu.VMEM((3, NZ, two, vec), F32),
            pltpu.VMEM((NZ, two, vec), F32),
            pltpu.VMEM((NZ, two, vec), F32),
            pltpu.VMEM((256, 2 * vec), F32),
            pltpu.VMEM((2, 2, NZ, 16, vec), F32),
            pltpu.VMEM((3, NZ, 16, vec), F32),
            pltpu.VMEM((NZ, 16, vec), F32),
            pltpu.VMEM((NZ, 16, vec), F32),
            pltpu.VMEM((16, half), F32),
            pltpu.VMEM((rows, half), BF16),
            pltpu.VMEM((16, half), BF16),
            pltpu.VMEM((256, 128), F32),
            pltpu.VMEM((vec, half), BF16),
            dma((2, 2, 4)), dma((2, NY)), dma((2, NY)), dma((2, NY)), dma((3,)), dma((3,)),
            dma((3, NZ)), dma((3, NZ)), dma((NZ,)), dma((NZ,)), dma((3,)), dma((3,)), dma((NZ,)), dma((NZ,)),
        ],
        compiler_params=pltpu.CompilerParams(
            collective_id=0, has_side_effects=True, vmem_limit_bytes=40 * 1024 * 1024
        ),
    )(cholesky, green_half, partners.T)


def solution(mesh):
    return jax.shard_map(
        local,
        mesh=mesh,
        in_specs=(P("loop", "orb"), P("loop", "orb"), P()),
        out_specs=(P("loop", "orb"), P("orb", "loop")),
        check_vma=False,
    )
```

time: 306 us -> 71.9 us (0.23)
  the two profiles are of different devices: /device:TPU:24 before, /device:TPU:4 now
where the time goes in v1:
time: 71.9 us; the launch traced here: 71.7 us
  Pallas kernels  66.7 us (93%)
  local copies, waits for them, and re-layouts  4.26 us (6%)
    pallas_call x1, Pallas kernels, local(): pl.pallas_call(kernel, out_shape=(jax.ShapeDtypeStruct((rows, depth), BF1...  66.7 us
    unnamed x8, local copies, waits for them, and re-layouts  4.26 us

profile of v1, /device:TPU:4, one launch (start us, length us, event | category | flops | bytes accessed | tf_op | source)
XLA Modules:
  0.0 71.7 jit_solution(2489604410470589316)
XLA Ops:
  0.6 0.0 copy-start
  0.6 1.2 %copy-done = bf16[128,4096]{1,0:T(8,128)(2,1)S(1)} copy-done((bf16[128,4096]{1,0:T(8,128)(2,1)S(1)}, bf16[128,4096]{1,0:T(8,128)(2,1)}, u32[]{:S(2)}) %copy-start) | copy-done | bytes 1048600
  1.9 0.0 copy-start.1
  1.9 1.0 %copy-done.1 = bf16[48,4096]{1,0:T(8,128)(2,1)S(1)} copy-done((bf16[48,4096]{1,0:T(8,128)(2,1)S(1)}, bf16[48,4096]{1,0:T(8,128)(2,1)}, u32[]{:S(2)}) %copy-start.1) | copy-done | bytes 393240
  2.9 0.0 copy-start.2
  2.9 0.7 copy-done.2
  3.5 66.7 %shard_map.50 = (bf16[48,4096]{1,0:T(8,128)(2,1)S(1)}, f32[96,128]{1,0:T(8,128)S(1)}) custom-call(bf16[128,4096]{1,0:T(8,128)(2,1)S(1)} %copy-done, bf16[48,4096]{1,0:T(8,128)(2,1)S(1)} %copy-done.1, s32[2,256]{1,0:T(2,128)S(1)} %bitcast.1), custom_call_target="tpu_custom_call" | custom-call | tf_op jit(solution)/shard_map/pallas_call | solution.py:325
  70.3 0.7 %copy.7 = bf16[48,4096]{1,0:T(8,128)(2,1)} copy(bf16[48,4096]{1,0:T(8,128)(2,1)S(1)} %get-tuple-element.4) | data formatting | bytes 786432
  71.0 0.6 copy.8
Async XLA Ops:
  0.6 1.2 %copy-start = (bf16[128,4096]{1,0:T(8,128)(2,1)S(1)}, bf16[128,4096]{1,0:T(8,128)(2,1)}, u32[]{:S(2)}) copy-start(bf16[128,4096]{1,0:T(8,128)(2,1)} %chol.1) | copy-start | bytes 3145732
  1.9 1.0 %copy-start.1 = (bf16[48,4096]{1,0:T(8,128)(2,1)S(1)}, bf16[48,4096]{1,0:T(8,128)(2,1)}, u32[]{:S(2)}) copy-start(bf16[48,4096]{1,0:T(8,128)(2,1)} %green.1) | copy-start | bytes 1179652
  2.9 0.7 copy-start.2

commit v2 on v1

v2 whole, which is shorter than its diff:
```python
import jax
import jax.numpy as jnp
from jax import lax
from jax.experimental import pallas as pl
from jax.experimental.pallas import tpu as pltpu
from jax.sharding import PartitionSpec as P

MESH = pl.DeviceIdType.MESH
NY, NZ, NX = 8, 8, 4
PER = 8
F32, BF16 = jnp.float32, jnp.bfloat16


def dot_t(a, b):
    return lax.dot_general(a, b, (((1,), (1,)), ((), ())), preferred_element_type=F32)


def split3(v):
    hi = v.astype(BF16)
    rest = v - hi.astype(F32)
    mid = rest.astype(BF16)
    lo = (rest - mid.astype(F32)).astype(BF16)
    return hi, mid, lo


def pick_rows(onehot, v):
    hi, mid, lo = split3(v)
    return (
        jnp.dot(onehot, hi, preferred_element_type=F32)
        + jnp.dot(onehot, mid, preferred_element_type=F32)
    ) + jnp.dot(onehot, lo, preferred_element_type=F32)


def iota(shape, dim):
    return lax.broadcasted_iota(jnp.int32, shape, dim).astype(F32)


def kernel(
    chol, green, prow, new_green, bias,
    gv, pv, gb, w, cs, rx, zs, rz, fix, fx, rfx, fzs, rfz, s_acc, s_out, s_in, q_out, dist, in_s,
    y_ss, y_rs, b_ss, b_rs, p_ss, p_rs, x_ss, x_rs, z_ss, z_rs, fx_ss, fx_rs, fz_ss, fz_rs, near,
):
    rows = green.shape[0]
    vec = chol.shape[0]
    half = green.shape[1] // 2
    part_k = half // 2
    kept = rows - PER
    two = 2 * kept
    events = prow.shape[1]
    loop, orb = lax.axis_index("loop"), lax.axis_index("orb")
    h, y, c = lax.div(loop, 16), lax.rem(lax.div(loop, 2), NY), lax.rem(loop, 2)
    z, xl = lax.div(orb, 2), lax.rem(orb, 2)
    x = 2 * h + xl
    other = 1 - h

    def dev(dx=0, dy=0, dz=0, dc=0):
        xx = lax.rem(x + dx, NX)
        yy = lax.rem(y + dy + NY, NY)
        zz = lax.rem(z + dz + NZ, NZ)
        cc = lax.rem(c + dc, 2)
        return (lax.div(xx, 2) * 16 + yy * 2 + cc, zz * 2 + lax.rem(xx, 2))

    def remote(src, dst, ss, rs, to):
        return pltpu.make_async_remote_copy(
            src_ref=src, dst_ref=dst, send_sem=ss, recv_sem=rs, device_id=to, device_id_type=MESH
        )

    def signal(sem, to):
        pl.semaphore_signal(sem, inc=1, device_id=to, device_id_type=MESH)

    own_cols = pl.ds(pl.multiple_of(h * half, half), half)
    far_cols = pl.ds(pl.multiple_of(other * half, half), half)
    w_own = w.at[pl.ds(pl.multiple_of(h * vec, vec), vec)]
    w_far = w.at[pl.ds(pl.multiple_of(other * vec, vec), vec)]
    p_in = pltpu.make_async_copy(prow, pv, in_s.at[0])
    g_in = pltpu.make_async_copy(green, gv, in_s.at[1])
    c_in = pltpu.make_async_copy(chol.at[:, own_cols], w_own, in_s.at[2])
    p_in.start()
    g_in.start()
    c_in.start()

    barrier = pltpu.get_barrier_semaphore()
    peers = [dev(dy=1), dev(dy=-1), dev(dc=1), dev(dz=1), dev(dz=-1)] + [dev(dx=k) for k in range(1, NX)]
    for peer in peers:
        signal(barrier, peer)

    def step_near(r):
        if r > 0:
            pl.semaphore_wait(near.at[r - 1], 2)
        if r < 3:
            signal(near.at[r], dev(dz=1))
            signal(near.at[r], dev(dz=-1))

    p_in.wait()
    src_row, tgt_row = pv[0:1, :].astype(F32), pv[1:2, :].astype(F32)

    def count(first, col):
        hit = jnp.sum(jnp.where(tgt_row == col, 1.0, 0.0), axis=1, keepdims=True)
        less = jnp.sum(jnp.where((tgt_row < col) & (tgt_row >= first), 1.0, 0.0), axis=1, keepdims=True)
        return hit > 0.5, less

    first = (loop * rows).astype(F32)
    local_row = iota((rows, 1), 0)
    hit, less = count(first, local_row + first)
    pack = jnp.where(jnp.logical_not(hit) & (local_row - less == iota((rows, kept), 1)), 1.0, 0.0).astype(BF16)

    def packed(cols):
        return lax.dot_general(
            pack, gv[:, cols], (((0,), (0,)), ((), ())), preferred_element_type=F32
        ).astype(BF16)

    g_in.wait()
    for k in range(2):
        gb[0, 0, k, c] = packed(pl.ds(pl.multiple_of(h * half + k * part_k, part_k), part_k))
        q_out[k] = packed(pl.ds(pl.multiple_of(other * half + k * part_k, part_k), part_k))
    pl.semaphore_wait(barrier, len(peers))

    def y_copy(pq, d, k, step):
        return remote(
            gb.at[pq, d % NY, k, c], gb.at[pq, (d - step) % NY, k, c],
            y_ss.at[pq, k, 0 if step > 0 else 1, abs(d)], y_rs.at[pq, (d - step) % NY, k], dev(dy=step),
        )

    def b_copy(pq, d, k):
        return remote(
            gb.at[pq, d % NY, k, c], gb.at[pq, d % NY, k, c], b_ss.at[pq, d % NY, k], b_rs.at[pq, d % NY, k], dev(dc=1)
        )

    def b_wait(pq, d, k):
        remote(
            gb.at[pq, d % NY, k, 1 - c], gb.at[pq, d % NY, k, 1 - c],
            b_ss.at[pq, d % NY, k], b_rs.at[pq, d % NY, k], dev(dc=1),
        ).wait_recv()

    def q_copy(k):
        return remote(q_out.at[k], gb.at[1, 0, k, c], p_ss.at[k], p_rs.at[k], dev(dx=2))

    started = []

    def go(copy):
        copy.start()
        started.append(copy)

    go(y_copy(0, 0, 0, 1))
    go(y_copy(0, 0, 1, -1))
    go(q_copy(0))
    go(q_copy(1))
    go(y_copy(0, 0, 1, 1))
    go(y_copy(0, 0, 0, -1))
    go(remote(chol.at[:, far_cols], w_own, p_ss.at[2], p_rs.at[2], dev(dx=2)))
    h_in = remote(chol.at[:, far_cols], w_far, p_ss.at[2], p_rs.at[2], dev(dx=2))
    step_near(0)
    go(b_copy(0, 0, 0))
    go(b_copy(0, 0, 1))

    diag = iota((events, events), 0) == iota((events, events), 1)
    tgt_col = jnp.sum(jnp.where(diag, tgt_row, 0.0), axis=1, keepdims=True)
    pos_row = jnp.sum(jnp.where(tgt_col < tgt_row, 1.0, 0.0), axis=0, keepdims=True)
    src_col = jnp.sum(jnp.where(iota((events, events), 0) == pos_row, src_row, 0.0), axis=1, keepdims=True)
    src_block = jnp.floor((src_col + 0.5) * (1.0 / rows))
    _, src_less = count(src_block * rows, src_col)
    src_kept = src_col - src_block * PER - src_less
    lane = iota((1, 3 * two), 1)
    lane = lane - jnp.where(lane >= two, 1.0 * two, 0.0) - jnp.where(lane >= 2 * two, 1.0 * two, 0.0)
    dist[...] = src_kept - lane
    fix[...] = jnp.zeros_like(fix)
    s_acc[...] = jnp.zeros_like(s_acc)

    parity_here = lax.rem(y + xl, 2)
    far_block = other * 16 + lax.rem(loop, 16)

    def place(pq, d):
        hb = h if pq == 0 else other
        yb = lax.rem(y + (d % NY), NY)
        return hb, yb, 4 * hb + lax.div(yb, 2)

    def x_copy(pq, d, dx, slot):
        to = lax.div(lax.rem(x + dx, NX), 2)
        return remote(
            cs.at[pq, d % NY, to], rx.at[dx - 1, slot], x_ss.at[dx - 1, slot], x_rs.at[dx - 1, slot], dev(dx=dx)
        )

    def compute(pq, d):
        hb, yb, slot = place(pq, d)
        blocks = []
        part = None
        for k in range(2):
            b_wait(pq, d, k)
            a = gb[pq, d % NY, k].reshape(two, part_k)
            blocks.append(a)
            term = dot_t(a, w[:, k * part_k : (k + 1) * part_k])
            part = term if part is None else part + term
        cs[pq, d % NY, 0] = part[:, :vec]
        cs[pq, d % NY, 1] = part[:, vec:]

        @pl.when(parity_here == d % 2)
        def _():
            x_copy(pq, d, 2, slot).start()

        @pl.when(parity_here != d % 2)
        def _():
            x_copy(pq, d, 1, slot).start()
            x_copy(pq, d, 3, slot).start()

        base = ((8 * hb + yb) * two).astype(F32)
        onehot = jnp.where(dist[...] == base, 1.0, 0.0).astype(BF16)
        fix[...] += jnp.dot(onehot, jnp.concatenate(split3(part), axis=0), preferred_element_type=F32)
        d_own = dist[pl.ds(pl.multiple_of(loop * PER, PER), PER), :]
        d_far = dist[pl.ds(pl.multiple_of(far_block * PER, PER), PER), :]
        d_both = jnp.concatenate([d_own, d_far], axis=0)[:, :two]
        onehot_s = jnp.where(d_both == base, 1.0, 0.0).astype(BF16)
        for k in range(2):
            s_acc[k] += jnp.dot(onehot_s, blocks[k], preferred_element_type=F32)

    def z_stage(pq, d):
        _, _, slot = place(pq, d)

        @pl.when(parity_here == d % 2)
        def _():
            for dx in range(1, NX):
                x_copy(pq, d, dx, slot).wait_recv()
            zs[slot] = (cs[pq, d % NY, h] + rx[0, slot]) + (rx[1, slot] + rx[2, slot])
            k = lax.rem(slot - z + NZ, NZ)

            @pl.when(k != 0)
            def _():
                remote(zs.at[slot], rz.at[k], z_ss.at[k], z_rs.at[k], dev(dz=k)).start()

    def take(pq, d, k):
        remote(
            gb.at[pq, d % NY, k, c], gb.at[pq, d % NY, k, c], y_ss.at[pq, k, 0, 0], y_rs.at[pq, d % NY, k], dev(dy=1)
        ).wait_recv()
        up_end, down_end = (4, 3) if k == 0 else (3, 4)
        if d < 0 and -d < up_end:
            go(y_copy(pq, d, k, 1))
        if 0 < d < down_end:
            go(y_copy(pq, d, k, -1))
        go(b_copy(pq, d, k))

    def enter(k):
        q_copy(k).wait_recv()
        go(y_copy(1, 0, k, 1))
        go(y_copy(1, 0, k, -1))
        go(b_copy(1, 0, k))

    take(0, -1, 0)
    take(0, 1, 1)
    enter(0)
    step_near(1)
    take(0, -1, 1)
    take(0, 1, 0)
    enter(1)
    step_near(2)
    take(0, -2, 0)
    take(0, 2, 1)
    take(1, -1, 0)
    take(1, 1, 0)
    step_near(3)
    take(1, -1, 1)
    take(1, 1, 1)
    take(0, -2, 1)
    take(0, 2, 0)
    take(1, -2, 0)
    take(0, 3, 1)
    take(0, -3, 0)
    take(1, 2, 1)
    c_in.wait()
    h_in.wait_recv()
    compute(0, 0)
    compute(1, 0)
    take(1, -2, 1)
    take(1, 2, 0)
    compute(0, -1)
    compute(0, 1)
    compute(1, -1)
    take(1, -3, 0)
    take(0, 3, 0)
    compute(1, 1)
    compute(0, -2)
    z_stage(0, 0)
    z_stage(1, 0)
    take(0, -3, 1)
    take(1, 3, 1)
    compute(0, 2)
    compute(1, -2)
    compute(1, 2)
    take(0, 4, 0)
    take(0, 4, 1)
    compute(0, -3)
    compute(0, 3)
    z_stage(0, -1)
    z_stage(0, 1)
    z_stage(1, -1)
    z_stage(1, 1)
    take(1, -3, 1)
    take(1, 3, 0)
    compute(0, 4)
    z_stage(0, -2)
    z_stage(0, 2)
    take(1, 4, 0)
    take(1, 4, 1)
    compute(1, -3)
    compute(1, 3)
    compute(1, 4)

    full = fix[...]
    for zz in range(NZ):
        for par in range(2):
            r0 = (2 * zz + par) * 16
            fx[par, 0, zz] = full[r0 : r0 + 16, :vec]
            fx[par, 1, zz] = full[r0 : r0 + 16, vec:]

    def fx_copy(dx):
        xx = lax.rem(x + dx, NX)
        return remote(fx.at[lax.rem(xx, 2), lax.div(xx, 2)], rfx.at[dx - 1], fx_ss.at[dx - 1], fx_rs.at[dx - 1], dev(dx=dx))

    for dx in range(1, NX):
        go(fx_copy(dx))
    for k in range(2):
        s_out[:, k * part_k : (k + 1) * part_k] = s_acc[k].astype(BF16)
    s_copy = remote(s_out, s_in, p_ss.at[3], p_rs.at[3], dev(dx=2))
    go(s_copy)
    for d in (-2, 2, -3, 3, 4):
        if abs(d) != 2:
            z_stage(0, d)
        z_stage(1, d)
    for dx in range(1, NX):
        fx_copy(dx).wait_recv()
    fzs[...] = (fx[xl, h] + rfx[0]) + (rfx[1] + rfx[2])

    def fz_copy(k):
        return remote(fzs.at[lax.rem(z + k, NZ)], rfz.at[k], fz_ss.at[k], fz_rs.at[k], dev(dz=k))

    for k in range(1, NZ):
        go(fz_copy(k))

    lane16 = iota((rows, 16), 1)
    put_own = jnp.where(hit & (less == lane16), 1.0, 0.0).astype(BF16)
    put_far = jnp.where(hit & (less + PER == lane16), 1.0, 0.0).astype(BF16)
    keep = jnp.where(jnp.logical_not(hit) & (local_row == iota((rows, rows), 1)), 1.0, 0.0).astype(BF16)
    new_green[:, own_cols] = (
        jnp.dot(keep, gv[:, own_cols], preferred_element_type=F32)
        + jnp.dot(put_own, s_out[...], preferred_element_type=F32)
    ).astype(BF16)
    s_copy.wait_recv()
    new_green[:, far_cols] = (
        jnp.dot(keep, gv[:, far_cols], preferred_element_type=F32)
        + jnp.dot(put_far, s_in[...], preferred_element_type=F32)
    ).astype(BF16)

    wide = 2 * rows
    o_first = (orb * wide).astype(F32)
    o_row = iota((wide, 1), 0)
    in_core = jnp.where(o_row >= rows, 1.0, 0.0)
    o_hit, o_less = count(o_first + in_core * rows, o_row + o_first)
    o_from = jnp.where(o_hit, two + in_core * PER + o_less, o_row - in_core * PER - o_less)
    order = jnp.where(o_from == iota((wide, wide), 1), 1.0, 0.0).astype(BF16)
    main = zs[z]
    tail = fzs[z]
    for k in range(1, NZ):
        remote(zs.at[0], rz.at[k], z_ss.at[k], z_rs.at[k], dev(dz=k)).wait_recv()
        main = main + rz[k]
    for k in range(1, NZ):
        fz_copy(k).wait_recv()
        tail = tail + rfz[k]
    bias[...] = pick_rows(order, jnp.concatenate([main, tail], axis=0))

    for copy in started:
        copy.wait_send()
    for dx in range(1, NX):
        for slot in range(NZ):
            remote(cs.at[0, 0, 0], rx.at[dx - 1, slot], x_ss.at[dx - 1, slot], x_rs.at[dx - 1, slot], dev(dx=dx)).wait_send()
    for k in range(1, NZ):
        remote(zs.at[0], rz.at[k], z_ss.at[k], z_rs.at[k], dev(dz=k)).wait_send()


def local(cholesky, green_half, partners):
    rows, depth = green_half.shape
    vec = cholesky.shape[0]
    half, two = depth // 2, 2 * (rows - PER)
    kept, part_k = rows - PER, half // 2
    dma = pltpu.SemaphoreType.DMA
    vmem = pl.BlockSpec(memory_space=pltpu.VMEM)
    hbm = pl.BlockSpec(memory_space=pl.ANY)
    return pl.pallas_call(
        kernel,
        out_shape=(
            jax.ShapeDtypeStruct((rows, depth), BF16),
            jax.ShapeDtypeStruct((2 * rows, vec), F32),
        ),
        in_specs=[hbm] * 3,
        out_specs=(vmem, vmem),
        scratch_shapes=[
            pltpu.VMEM((rows, depth), BF16),
            pltpu.VMEM((2, 256), jnp.int32),
            pltpu.VMEM((2, NY, 2, 2, kept, part_k), BF16),
            pltpu.VMEM((2 * vec, half), BF16),
            pltpu.VMEM((2, NY, 2, two, vec), F32),
            pltpu.VMEM((3, NZ, two, vec), F32),
            pltpu.VMEM((NZ, two, vec), F32),
            pltpu.VMEM((NZ, two, vec), F32),
            pltpu.VMEM((256, 2 * vec), F32),
            pltpu.VMEM((2, 2, NZ, 16, vec), F32),
            pltpu.VMEM((3, NZ, 16, vec), F32),
            pltpu.VMEM((NZ, 16, vec), F32),
            pltpu.VMEM((NZ, 16, vec), F32),
            pltpu.VMEM((2, 16, part_k), F32),
            pltpu.VMEM((16, half), BF16),
            pltpu.VMEM((16, half), BF16),
            pltpu.VMEM((2, kept, part_k), BF16),
            pltpu.VMEM((256, 3 * two), F32),
            dma((3,)),
            dma((2, 2, 2, 4)), dma((2, NY, 2)), dma((2, NY, 2)), dma((2, NY, 2)), dma((4,)), dma((4,)),
            dma((3, NZ)), dma((3, NZ)), dma((NZ,)), dma((NZ,)), dma((3,)), dma((3,)), dma((NZ,)), dma((NZ,)),
            pltpu.SemaphoreType.REGULAR((3,)),
        ],
        compiler_params=pltpu.CompilerParams(
            collective_id=0, has_side_effects=True, vmem_limit_bytes=60 * 1024 * 1024
        ),
    )(cholesky, green_half, partners.T)


def solution(mesh):
    return jax.shard_map(
        local,
        mesh=mesh,
        in_specs=(P("loop", "orb"), P("loop", "orb"), P()),
        out_specs=(P("loop", "orb"), P("orb", "loop")),
        check_vma=False,
    )
```

time: 71.9 us -> 66.3 us (0.922)
  the two profiles are of different devices: /device:TPU:4 before, /device:TPU:22 now
where the time goes in v2:
time: 66.3 us; the launch traced here: 66.2 us
  Pallas kernels  63.1 us (95%)
  local copies, waits for them, and re-layouts  2.4 us (4%)
    pallas_call x1, Pallas kernels, local(): pl.pallas_call(kernel, out_shape=(jax.ShapeDtypeStruct((rows, depth), BF1...  63.1 us
    unnamed x4, local copies, waits for them, and re-layouts  2.4 us

profile of v2, /device:TPU:22, one launch (start us, length us, event | category | flops | bytes accessed | tf_op | source)
XLA Modules:
  0.0 66.2 jit_solution(10166388051034169148)
XLA Ops:
  0.6 63.1 %shard_map.50 = (bf16[48,4096]{1,0:T(8,128)(2,1)}, f32[96,128]{1,0:T(8,128)}) custom-call(bf16[128,4096]{1,0:T(8,128)(2,1)} %chol.1, bf16[48,4096]{1,0:T(8,128)(2,1)} %green.1, s32[2,256]{1,0:T(2,128)} %bitcast.1), custom_call_target="tpu_custom_call" | custom-call | tf_op jit(solution)/shard_map/pallas_call | solution.py:385
  63.7 0.0 copy-start
  63.8 1.8 %copy.7 = bf16[48,4096]{1,0:T(8,128)(2,1)} copy(bf16[48,4096]{1,0:T(8,128)(2,1)} %get-tuple-element.4) | data formatting | bytes 786432
  65.5 0.0 copy-done
  65.5 0.6 copy.8
Async XLA Ops:
  63.7 1.8 %copy-start = (f32[96,128]{1,0:T(8,128)S(1)}, f32[96,128]{1,0:T(8,128)}, u32[]{:S(2)}) copy-start(f32[96,128]{1,0:T(8,128)} %get-tuple-element.5) | copy-start | bytes 147460

commit v3 on v2

v3 whole, which is shorter than its diff:
```python
import jax
import jax.numpy as jnp
from jax import lax
from jax.experimental import pallas as pl
from jax.experimental.pallas import tpu as pltpu
from jax.sharding import PartitionSpec as P

MESH = pl.DeviceIdType.MESH
NY, NZ, NX = 8, 8, 4
PER = 8
F32, BF16 = jnp.float32, jnp.bfloat16


def dot_t(a, b):
    return lax.dot_general(a, b, (((1,), (1,)), ((), ())), preferred_element_type=F32)


def split3(v):
    hi = v.astype(BF16)
    rest = v - hi.astype(F32)
    mid = rest.astype(BF16)
    lo = (rest - mid.astype(F32)).astype(BF16)
    return hi, mid, lo


def pick_rows(onehot, v):
    hi, mid, lo = split3(v)
    return (
        jnp.dot(onehot, hi, preferred_element_type=F32)
        + jnp.dot(onehot, mid, preferred_element_type=F32)
    ) + jnp.dot(onehot, lo, preferred_element_type=F32)


def iota(shape, dim):
    return lax.broadcasted_iota(jnp.int32, shape, dim).astype(F32)


def kernel(
    chol, green, prow, new_green, bias,
    gv, pv, ga, gb, w, cs, rx, zs, rz, fs, rfs, fss, rfsz, fd, rfd, fdd, rfdx, ng, s_out, s_in, qa_out, qb_out, c_src, rel, in_s,
    y_ss, y_rs, b_ss, b_rs, p_ss, p_rs, x_ss, x_rs, z_ss, z_rs, e_ss, e_rs, near,
):
    rows = green.shape[0]
    vec = chol.shape[0]
    half = green.shape[1] // 2
    part_k = half // 2
    kept = rows - 2 * PER
    two = 2 * kept
    events = prow.shape[1]
    loop, orb = lax.axis_index("loop"), lax.axis_index("orb")
    h, y, c = lax.div(loop, 16), lax.rem(lax.div(loop, 2), NY), lax.rem(loop, 2)
    z, xl = lax.div(orb, 2), lax.rem(orb, 2)
    x = 2 * h + xl
    other = 1 - h

    def dev(dx=0, dy=0, dz=0, dc=0):
        xx = lax.rem(x + dx, NX)
        yy = lax.rem(y + dy + NY, NY)
        zz = lax.rem(z + dz + NZ, NZ)
        cc = lax.rem(c + dc, 2)
        return (lax.div(xx, 2) * 16 + yy * 2 + cc, zz * 2 + lax.rem(xx, 2))

    def remote(src, dst, ss, rs, to):
        return pltpu.make_async_remote_copy(
            src_ref=src, dst_ref=dst, send_sem=ss, recv_sem=rs, device_id=to, device_id_type=MESH
        )

    def signal(sem, to):
        pl.semaphore_signal(sem, inc=1, device_id=to, device_id_type=MESH)

    own_cols = pl.ds(pl.multiple_of(h * half, half), half)
    far_cols = pl.ds(pl.multiple_of(other * half, half), half)
    w_own = w.at[pl.ds(pl.multiple_of(h * vec, vec), vec)]
    w_far = w.at[pl.ds(pl.multiple_of(other * vec, vec), vec)]
    p_in = pltpu.make_async_copy(prow, pv, in_s.at[0])
    g_in = pltpu.make_async_copy(green, gv, in_s.at[1])
    c_in = pltpu.make_async_copy(chol.at[:, own_cols], w_own, in_s.at[2])
    p_in.start()
    g_in.start()
    c_in.start()

    barrier = pltpu.get_barrier_semaphore()
    peers = [dev(dy=1), dev(dy=-1), dev(dc=1), dev(dz=1), dev(dz=-1)] + [dev(dx=k) for k in range(1, NX)]
    for peer in peers:
        signal(barrier, peer)

    def step_near(r):
        if r > 0:
            pl.semaphore_wait(near.at[r - 1], 2)
        if r < 3:
            signal(near.at[r], dev(dz=1))
            signal(near.at[r], dev(dz=-1))

    p_in.wait()
    src_row, tgt_row = pv[0:1, :].astype(F32), pv[1:2, :].astype(F32)

    def count(row, first, col):
        hit = jnp.sum(jnp.where(row == col, 1.0, 0.0), axis=1, keepdims=True)
        less = jnp.sum(jnp.where((row < col) & (row >= first), 1.0, 0.0), axis=1, keepdims=True)
        return hit, less

    first = (loop * rows).astype(F32)
    local_row = iota((rows, 1), 0)
    hit_t, less = count(tgt_row, first, local_row + first)
    hit_s, less_s = count(src_row, first, local_row + first)
    hit = hit_t > 0.5
    pack_a = jnp.where((hit_s > 0.5) & (less_s == iota((rows, PER), 1)), 1.0, 0.0).astype(BF16)
    pack_b = jnp.where(
        (hit_s + hit_t < 0.5) & (local_row - less - less_s == iota((rows, kept), 1)), 1.0, 0.0
    ).astype(BF16)

    def packed(pack, which, k):
        cols = pl.ds(pl.multiple_of(which * half + k * part_k, part_k), part_k)
        return lax.dot_general(pack, gv[:, cols], (((0,), (0,)), ((), ())), preferred_element_type=F32)

    def chunk(pq, d, kind, core):
        return ga.at[pq, d % NY, core] if kind == 2 else gb.at[pq, d % NY, kind, core]

    def y_copy(pq, d, kind, step):
        return remote(
            chunk(pq, d, kind, c), chunk(pq, d - step, kind, c),
            y_ss.at[pq, kind, 0 if step > 0 else 1, abs(d)], y_rs.at[pq, (d - step) % NY, kind], dev(dy=step),
        )

    def b_copy(pq, d, kind):
        return remote(
            chunk(pq, d, kind, c), chunk(pq, d, kind, c), b_ss.at[pq, d % NY, kind], b_rs.at[pq, d % NY, kind], dev(dc=1)
        )

    def b_wait(pq, d, kind):
        remote(
            chunk(pq, d, kind, 1 - c), chunk(pq, d, kind, 1 - c),
            b_ss.at[pq, d % NY, kind], b_rs.at[pq, d % NY, kind], dev(dc=1),
        ).wait_recv()

    def q_copy(kind):
        src = qa_out if kind == 2 else qb_out.at[kind]
        return remote(src, chunk(1, 0, kind, c), p_ss.at[kind], p_rs.at[kind], dev(dx=2))

    started = []

    def go(copy):
        copy.start()
        started.append(copy)

    g_in.wait()
    ga[0, 0, c] = jnp.concatenate([packed(pack_a, h, k) for k in range(2)], axis=0).astype(BF16)
    gb[0, 0, 0, c] = packed(pack_b, h, 0).astype(BF16)
    pl.semaphore_wait(barrier, len(peers))
    go(y_copy(0, 0, 2, 1))
    go(y_copy(0, 0, 2, -1))
    go(y_copy(0, 0, 0, 1))
    gb[0, 0, 1, c] = packed(pack_b, h, 1).astype(BF16)
    go(y_copy(0, 0, 1, -1))
    qa_out[...] = jnp.concatenate([packed(pack_a, other, k) for k in range(2)], axis=0).astype(BF16)
    go(q_copy(2))
    qb_out[0] = packed(pack_b, other, 0).astype(BF16)
    go(q_copy(0))
    go(y_copy(0, 0, 1, 1))
    go(y_copy(0, 0, 0, -1))
    qb_out[1] = packed(pack_b, other, 1).astype(BF16)
    go(q_copy(1))
    go(remote(chol.at[:, far_cols], w_own, p_ss.at[3], p_rs.at[3], dev(dx=2)))
    h_in = remote(chol.at[:, far_cols], w_far, p_ss.at[3], p_rs.at[3], dev(dx=2))
    step_near(0)
    for kind in (2, 0, 1):
        go(b_copy(0, 0, kind))

    diag = iota((events, events), 0) == iota((events, events), 1)
    tgt_col = jnp.sum(jnp.where(diag, tgt_row, 0.0), axis=1, keepdims=True)
    pos_row = jnp.sum(jnp.where(tgt_col < tgt_row, 1.0, 0.0), axis=0, keepdims=True)
    src_col = jnp.sum(jnp.where(iota((events, events), 0) == pos_row, src_row, 0.0), axis=1, keepdims=True)
    src_block = jnp.floor((src_col + 0.5) * (1.0 / rows))
    _, rank = count(src_row, src_block * rows, src_col)
    src_h = jnp.floor((src_block + 0.5) * (1.0 / 16))
    src_y = jnp.floor((src_block - 16.0 * src_h + 0.5) * 0.5)
    src_c = src_block - 16.0 * src_h - 2.0 * src_y
    src_d = src_y - y.astype(F32)
    src_d = src_d + jnp.where(src_d < 0.0, 1.0 * NY, 0.0)
    src_at = 2.0 * (NY * jnp.abs(src_h - h.astype(F32)) + src_d) + src_c
    rel[...] = jnp.broadcast_to(src_at * (2 * PER) + rank, rel.shape)

    parity_here = lax.rem(y + xl, 2)
    far_block = other * 16 + lax.rem(loop, 16)

    def place(pq, d):
        hb = h if pq == 0 else other
        yb = lax.rem(y + (d % NY), NY)
        return hb, yb, 4 * hb + lax.div(yb, 2)

    def x_copy(pq, d, dx, slot):
        to = lax.div(lax.rem(x + dx, NX), 2)
        return remote(
            cs.at[pq, d % NY, to], rx.at[dx - 1, slot], x_ss.at[dx - 1, slot], x_rs.at[dx - 1, slot], dev(dx=dx)
        )

    def compute(pq, d):
        _, _, slot = place(pq, d)
        part = None
        for k in range(2):
            b_wait(pq, d, k)
            term = dot_t(gb[pq, d % NY, k].reshape(two, part_k), w[:, k * part_k : (k + 1) * part_k])
            part = term if part is None else part + term
        cs[pq, d % NY, 0] = part[:, :vec]
        cs[pq, d % NY, 1] = part[:, vec:]

        @pl.when(parity_here == d % 2)
        def _():
            x_copy(pq, d, 2, slot).start()

        @pl.when(parity_here != d % 2)
        def _():
            x_copy(pq, d, 1, slot).start()
            x_copy(pq, d, 3, slot).start()

    def z_stage(pq, d):
        _, _, slot = place(pq, d)

        @pl.when(parity_here == d % 2)
        def _():
            for dx in range(1, NX):
                x_copy(pq, d, dx, slot).wait_recv()
            zs[slot] = (cs[pq, d % NY, h] + rx[0, slot]) + (rx[1, slot] + rx[2, slot])
            k = lax.rem(slot - z + NZ, NZ)

            @pl.when(k != 0)
            def _():
                remote(zs.at[slot], rz.at[k], z_ss.at[k], z_rs.at[k], dev(dz=k)).start()

    def take(pq, d, kind):
        remote(
            chunk(pq, d, kind, c), chunk(pq, d, kind, c), y_ss.at[pq, kind, 0, 0], y_rs.at[pq, d % NY, kind], dev(dy=1)
        ).wait_recv()
        long_up = kind == 0 or (kind == 2 and pq == 0)
        up_end, down_end = (4, 3) if long_up else (3, 4)
        if d < 0 and -d < up_end:
            go(y_copy(pq, d, kind, 1))
        if 0 < d < down_end:
            go(y_copy(pq, d, kind, -1))
        go(b_copy(pq, d, kind))

    def enter(kind):
        q_copy(kind).wait_recv()
        go(y_copy(1, 0, kind, 1))
        go(y_copy(1, 0, kind, -1))
        go(b_copy(1, 0, kind))

    def source_parts():
        both = 2 * PER
        for pq in range(2):
            for d in range(NY):
                b_wait(pq, d, 2)
        a = ga[...].reshape(2 * NY * 2 * both, part_k)
        t = [dot_t(a, w[:, k * part_k : (k + 1) * part_k]).reshape(4 * NY, both, 2 * vec) for k in range(2)]
        c_src[...] = (t[0][:, :PER] + t[1][:, PER:]).reshape(4 * NY * PER, 2 * vec)

    def fs_x(dx):
        xx = lax.rem(x + dx, NX)
        return remote(fs.at[lax.rem(xx, 2), lax.div(xx, 2)], rfs.at[dx - 1], e_ss.at[0, dx], e_rs.at[0, dx], dev(dx=dx))

    def fs_z(k):
        return remote(fss.at[lax.rem(z + k, NZ)], rfsz.at[k], e_ss.at[1, k], e_rs.at[1, k], dev(dz=k))

    def fd_z(k):
        return remote(fd.at[lax.rem(z + k, NZ)], rfd.at[k], e_ss.at[2, k], e_rs.at[2, k], dev(dz=k))

    def fd_x(dx):
        xx = lax.rem(x + dx, NX)
        return remote(fdd.at[lax.rem(xx, 2), lax.div(xx, 2)], rfdx.at[dx - 1], e_ss.at[3, dx], e_rs.at[3, dx], dev(dx=dx))

    def source_send():
        sums = c_src[...]
        both = 2 * PER
        for pq in range(2):
            for d in range(NY):
                _, yb, slot = place(pq, d)
                r0 = (pq * NY + d) * both
                for g in range(2):
                    fs[lax.rem(yb, 2), g, slot] = sums[r0 : r0 + both, g * vec : (g + 1) * vec]
        for dx in range(1, NX):
            go(fs_x(dx))
        block = jnp.floor((rel[:, 0:1] + 0.5) * (1.0 / (2 * PER)))
        at = rel[:, 0:1] - PER * block
        picked = pick_rows(jnp.where(at == iota((events, events), 1), 1.0, 0.0).astype(BF16), sums)
        for zz in range(NZ):
            for par in range(2):
                r0 = (2 * zz + par) * both
                for g in range(2):
                    fd[zz, par, g] = picked[r0 : r0 + both, g * vec : (g + 1) * vec]
        for k in range(1, NZ):
            go(fd_z(k))

    s_copy = remote(s_out, s_in, p_ss.at[4], p_rs.at[4], dev(dx=2))

    def rows_send():
        here = rel[pl.ds(pl.multiple_of(loop * PER, PER), PER), :]
        there = rel[pl.ds(pl.multiple_of(far_block * PER, PER), PER), :]
        at = jnp.concatenate([here, there], axis=0)[:, 0:1]
        a = ga[...].reshape(8 * NY * PER, part_k)
        for k in range(2):
            onehot = jnp.where(at + k * PER == iota((2 * PER, 8 * NY * PER), 1), 1.0, 0.0).astype(BF16)
            s_out[:, k * part_k : (k + 1) * part_k] = jnp.dot(onehot, a, preferred_element_type=F32).astype(BF16)
        go(s_copy)

    g_out = pltpu.make_async_copy(ng, new_green, in_s.at[3])

    def rows_out():
        s_copy.wait_recv()
        lane16 = iota((rows, 2 * PER), 1)
        put_own = jnp.where(hit & (less == lane16), 1.0, 0.0).astype(BF16)
        put_far = jnp.where(hit & (less + PER == lane16), 1.0, 0.0).astype(BF16)
        keep = jnp.where(jnp.logical_not(hit) & (local_row == iota((rows, rows), 1)), 1.0, 0.0).astype(BF16)
        for cols, put, got in ((own_cols, put_own, s_out), (far_cols, put_far, s_in)):
            ng[:, cols] = (
                jnp.dot(keep, gv[:, cols], preferred_element_type=F32)
                + jnp.dot(put, got[...], preferred_element_type=F32)
            ).astype(BF16)
        g_out.start()

    def sources_on():
        for dx in range(1, NX):
            fs_x(dx).wait_recv()
        fss[...] = (fs[xl, h] + rfs[0]) + (rfs[1] + rfs[2])
        for k in range(1, NZ):
            go(fs_z(k))

    def destinations_on():
        total = fd[z]
        for k in range(1, NZ):
            fd_z(k).wait_recv()
            total = total + rfd[k]
        fdd[...] = total
        for dx in range(1, NX):
            go(fd_x(dx))

    def takes(*items):
        for item in items:
            take(*item)

    takes((0, -1, 2), (0, 1, 2))
    enter(2)
    takes((0, -1, 0), (0, 1, 1))
    step_near(1)
    enter(0)
    takes((0, -1, 1), (0, 1, 0), (0, -2, 2), (0, 2, 2))
    enter(1)
    step_near(2)
    takes((1, -1, 2), (1, 1, 2), (0, -2, 0), (0, 2, 1), (1, -1, 0), (1, 1, 0))
    step_near(3)
    takes((0, -3, 2), (0, 3, 2), (1, -2, 2), (1, 2, 2), (1, -1, 1), (1, 1, 1), (0, -2, 1), (0, 2, 0))
    c_in.wait()
    h_in.wait_recv()
    compute(0, 0)
    takes((0, 4, 2), (0, 3, 1))
    compute(1, 0)
    takes((1, -3, 2), (1, 3, 2))
    compute(0, -1)
    takes((1, -2, 0), (1, 2, 1))
    compute(0, 1)
    takes((0, -3, 0), (1, 2, 0))
    compute(1, -1)
    takes((1, 4, 2), (1, -2, 1), (0, 3, 0))
    compute(1, 1)
    source_parts()
    source_send()
    takes((0, -3, 1), (1, -3, 0), (1, 3, 1))
    for d in (-2, 2):
        compute(0, d)
    for d in (-2, 2):
        compute(1, d)
    takes((0, 4, 0), (0, 4, 1))
    for d in (-3, 3):
        compute(0, d)
    compute(0, 4)
    takes((1, -3, 1), (1, 3, 0))
    rows_send()
    for d in (0, -1, 1):
        z_stage(0, d)
        z_stage(1, d)
    for d in (-3, 3):
        compute(1, d)
    takes((1, 4, 0), (1, 4, 1))
    compute(1, 4)
    sources_on()
    for d in (-2, 2, -3, 3, 4):
        z_stage(0, d)
        z_stage(1, d)
    destinations_on()
    rows_out()

    wide = 2 * rows
    o_first = (orb * wide).astype(F32)
    o_row = iota((wide, 1), 0)
    in_core = jnp.where(o_row >= rows, 1.0, 0.0)
    o_base, o_abs = o_first + in_core * rows, o_row + o_first
    hit_o, t_less = count(tgt_row, o_base, o_abs)
    hit_i, s_less = count(src_row, o_base, o_abs)
    o_from = o_row - in_core * (rows - kept) - t_less - s_less
    o_from = jnp.where(hit_i > 0.5, two + in_core * PER + s_less, o_from)
    o_from = jnp.where(hit_o > 0.5, two + (2 + in_core) * PER + t_less, o_from)
    order = jnp.where(o_from == iota((wide, wide), 1), 1.0, 0.0).astype(BF16)
    main, from_s, from_d = zs[z], fss[z], fdd[xl, h]
    for dx in range(1, NX):
        fd_x(dx).wait_recv()
        from_d = from_d + rfdx[dx - 1]
    for k in range(1, NZ):
        fs_z(k).wait_recv()
        from_s = from_s + rfsz[k]
    for k in range(1, NZ):
        remote(zs.at[0], rz.at[k], z_ss.at[k], z_rs.at[k], dev(dz=k)).wait_recv()
        main = main + rz[k]
    bias[...] = pick_rows(order, jnp.concatenate([main, from_s, from_d], axis=0))

    g_out.wait()
    for copy in started:
        copy.wait_send()
    for dx in range(1, NX):
        for slot in range(NZ):
            remote(cs.at[0, 0, 0], rx.at[dx - 1, slot], x_ss.at[dx - 1, slot], x_rs.at[dx - 1, slot], dev(dx=dx)).wait_send()
    for k in range(1, NZ):
        remote(zs.at[0], rz.at[k], z_ss.at[k], z_rs.at[k], dev(dz=k)).wait_send()


def local(cholesky, green_half, partners):
    rows, depth = green_half.shape
    vec = cholesky.shape[0]
    half, kept = depth // 2, rows - 2 * PER
    two, part_k, both = 2 * kept, half // 2, 2 * PER
    dma = pltpu.SemaphoreType.DMA
    vmem = pl.BlockSpec(memory_space=pltpu.VMEM)
    hbm = pl.BlockSpec(memory_space=pl.ANY)
    return pl.pallas_call(
        kernel,
        out_shape=(
            jax.ShapeDtypeStruct((rows, depth), BF16),
            jax.ShapeDtypeStruct((2 * rows, vec), F32),
        ),
        in_specs=[hbm] * 3,
        out_specs=(hbm, vmem),
        scratch_shapes=[
            pltpu.VMEM((rows, depth), BF16),
            pltpu.VMEM((2, 256), jnp.int32),
            pltpu.VMEM((2, NY, 2, both, part_k), BF16),
            pltpu.VMEM((2, NY, 2, 2, kept, part_k), BF16),
            pltpu.VMEM((2 * vec, half), BF16),
            pltpu.VMEM((2, NY, 2, two, vec), F32),
            pltpu.VMEM((3, NZ, two, vec), F32),
            pltpu.VMEM((NZ, two, vec), F32),
            pltpu.VMEM((NZ, two, vec), F32),
            pltpu.VMEM((2, 2, NZ, both, vec), F32),
            pltpu.VMEM((3, NZ, both, vec), F32),
            pltpu.VMEM((NZ, both, vec), F32),
            pltpu.VMEM((NZ, both, vec), F32),
            pltpu.VMEM((NZ, 2, 2, both, vec), F32),
            pltpu.VMEM((NZ, 2, 2, both, vec), F32),
            pltpu.VMEM((2, 2, both, vec), F32),
            pltpu.VMEM((3, both, vec), F32),
            pltpu.VMEM((rows, depth), BF16),
            pltpu.VMEM((both, half), BF16),
            pltpu.VMEM((both, half), BF16),
            pltpu.VMEM((both, part_k), BF16),
            pltpu.VMEM((2, kept, part_k), BF16),
            pltpu.VMEM((256, 2 * vec), F32),
            pltpu.VMEM((256, 128), F32),
            dma((4,)),
            dma((2, 3, 2, 4)), dma((2, NY, 3)), dma((2, NY, 3)), dma((2, NY, 3)), dma((5,)), dma((5,)),
            dma((3, NZ)), dma((3, NZ)), dma((NZ,)), dma((NZ,)), dma((4, NZ)), dma((4, NZ)),
            pltpu.SemaphoreType.REGULAR((3,)),
        ],
        compiler_params=pltpu.CompilerParams(
            collective_id=0, has_side_effects=True, vmem_limit_bytes=60 * 1024 * 1024
        ),
    )(cholesky, green_half, partners.T)


def solution(mesh):
    return jax.shard_map(
        local,
        mesh=mesh,
        in_specs=(P("loop", "orb"), P("loop", "orb"), P()),
        out_specs=(P("loop", "orb"), P("orb", "loop")),
        check_vma=False,
    )
```

time: 66.3 us -> 64.1 us (0.967)
  the two profiles are of different devices: /device:TPU:22 before, /device:TPU:24 now
where the time goes in v3:
time: 64.1 us; the launch traced here: 63.9 us
  Pallas kernels  60.9 us (95%)
  local copies, waits for them, and re-layouts  2.4 us (4%)
  between operations  0.65 us (1%)
    pallas_call x1, Pallas kernels, local(): pl.pallas_call(kernel, out_shape=(jax.ShapeDtypeStruct((rows, depth), BF1...  60.9 us
    unnamed x4, local copies, waits for them, and re-layouts  2.4 us

profile of v3, /device:TPU:24, one launch (start us, length us, event | category | flops | bytes accessed | tf_op | source)
XLA Modules:
  0.0 63.9 jit_solution(5238686569192142794)
XLA Ops:
  0.6 60.9 %shard_map.50 = (bf16[48,4096]{1,0:T(8,128)(2,1)}, f32[96,128]{1,0:T(8,128)}) custom-call(bf16[128,4096]{1,0:T(8,128)(2,1)} %chol.1, bf16[48,4096]{1,0:T(8,128)(2,1)} %green.1, s32[2,256]{1,0:T(2,128)} %bitcast.1), custom_call_target="tpu_custom_call" | custom-call | tf_op jit(solution)/shard_map/pallas_call | solution.py:432
  61.5 0.0 copy-start
  61.5 1.8 %copy.7 = bf16[48,4096]{1,0:T(8,128)(2,1)} copy(bf16[48,4096]{1,0:T(8,128)(2,1)} %get-tuple-element.4) | data formatting | bytes 786432
  63.3 0.0 copy-done
  63.3 0.6 copy.8
Async XLA Ops:
  61.5 1.8 %copy-start = (f32[96,128]{1,0:T(8,128)S(1)}, f32[96,128]{1,0:T(8,128)}, u32[]{:S(2)}) copy-start(f32[96,128]{1,0:T(8,128)} %get-tuple-element.5) | copy-start | bytes 147460

commit v4 on v3

--- a/solution.py
+++ b/solution.py
@@ -119,19 +119,17 @@
     def y_copy(pq, d, kind, step):
         return remote(
             chunk(pq, d, kind, c), chunk(pq, d - step, kind, c),
-            y_ss.at[pq, kind, 0 if step > 0 else 1, abs(d)], y_rs.at[pq, (d - step) % NY, kind], dev(dy=step),
+            y_ss.at[kind], y_rs.at[pq, (d - step) % NY, kind], dev(dy=step),
         )
 
     def b_copy(pq, d, kind):
         return remote(
-            chunk(pq, d, kind, c), chunk(pq, d, kind, c), b_ss.at[pq, d % NY, kind], b_rs.at[pq, d % NY, kind], dev(dc=1)
+            chunk(pq, d, kind, c), chunk(pq, d, kind, c),
+            b_ss.at[kind // 2], b_rs.at[2 * NY if kind == 2 else pq * NY + d % NY], dev(dc=1),
         )
 
-    def b_wait(pq, d, kind):
-        remote(
-            chunk(pq, d, kind, 1 - c), chunk(pq, d, kind, 1 - c),
-            b_ss.at[pq, d % NY, kind], b_rs.at[pq, d % NY, kind], dev(dc=1),
-        ).wait_recv()
+    def all_of(ref, ss, rs):
+        return remote(ref, ref, ss, rs, dev(dc=1))
 
     def q_copy(kind):
         src = qa_out if kind == 2 else qb_out.at[kind]
@@ -147,24 +145,24 @@
     ga[0, 0, c] = jnp.concatenate([packed(pack_a, h, k) for k in range(2)], axis=0).astype(BF16)
     gb[0, 0, 0, c] = packed(pack_b, h, 0).astype(BF16)
     pl.semaphore_wait(barrier, len(peers))
-    go(y_copy(0, 0, 2, 1))
-    go(y_copy(0, 0, 2, -1))
-    go(y_copy(0, 0, 0, 1))
+    y_copy(0, 0, 2, 1).start()
+    y_copy(0, 0, 2, -1).start()
+    y_copy(0, 0, 0, 1).start()
     gb[0, 0, 1, c] = packed(pack_b, h, 1).astype(BF16)
-    go(y_copy(0, 0, 1, -1))
+    y_copy(0, 0, 1, -1).start()
     qa_out[...] = jnp.concatenate([packed(pack_a, other, k) for k in range(2)], axis=0).astype(BF16)
     go(q_copy(2))
     qb_out[0] = packed(pack_b, other, 0).astype(BF16)
     go(q_copy(0))
-    go(y_copy(0, 0, 1, 1))
-    go(y_copy(0, 0, 0, -1))
+    y_copy(0, 0, 1, 1).start()
+    y_copy(0, 0, 0, -1).start()
     qb_out[1] = packed(pack_b, other, 1).astype(BF16)
     go(q_copy(1))
     go(remote(chol.at[:, far_cols], w_own, p_ss.at[3], p_rs.at[3], dev(dx=2)))
     h_in = remote(chol.at[:, far_cols], w_far, p_ss.at[3], p_rs.at[3], dev(dx=2))
     step_near(0)
     for kind in (2, 0, 1):
-        go(b_copy(0, 0, kind))
+        b_copy(0, 0, kind).start()
 
     diag = iota((events, events), 0) == iota((events, events), 1)
     tgt_col = jnp.sum(jnp.where(diag, tgt_row, 0.0), axis=1, keepdims=True)
@@ -191,14 +189,14 @@
     def x_copy(pq, d, dx, slot):
         to = lax.div(lax.rem(x + dx, NX), 2)
         return remote(
-            cs.at[pq, d % NY, to], rx.at[dx - 1, slot], x_ss.at[dx - 1, slot], x_rs.at[dx - 1, slot], dev(dx=dx)
+            cs.at[pq, d % NY, to], rx.at[dx - 1, slot], x_ss.at[0], x_rs.at[slot], dev(dx=dx)
         )
 
     def compute(pq, d):
         _, _, slot = place(pq, d)
         part = None
+        all_of(gb.at[pq, d % NY, :, 1 - c], b_ss.at[0], b_rs.at[pq * NY + d % NY]).wait_recv()
         for k in range(2):
-            b_wait(pq, d, k)
             term = dot_t(gb[pq, d % NY, k].reshape(two, part_k), w[:, k * part_k : (k + 1) * part_k])
             part = term if part is None else part + term
         cs[pq, d % NY, 0] = part[:, :vec]
@@ -218,55 +216,52 @@
 
         @pl.when(parity_here == d % 2)
         def _():
-            for dx in range(1, NX):
-                x_copy(pq, d, dx, slot).wait_recv()
+            all_of(rx.at[:, slot], x_ss.at[0], x_rs.at[slot]).wait_recv()
             zs[slot] = (cs[pq, d % NY, h] + rx[0, slot]) + (rx[1, slot] + rx[2, slot])
             k = lax.rem(slot - z + NZ, NZ)
 
             @pl.when(k != 0)
             def _():
-                remote(zs.at[slot], rz.at[k], z_ss.at[k], z_rs.at[k], dev(dz=k)).start()
+                remote(zs.at[slot], rz.at[k], z_ss.at[0], z_rs.at[0], dev(dz=k)).start()
 
     def take(pq, d, kind):
         remote(
-            chunk(pq, d, kind, c), chunk(pq, d, kind, c), y_ss.at[pq, kind, 0, 0], y_rs.at[pq, d % NY, kind], dev(dy=1)
+            chunk(pq, d, kind, c), chunk(pq, d, kind, c), y_ss.at[kind], y_rs.at[pq, d % NY, kind], dev(dy=1)
         ).wait_recv()
         long_up = kind == 0 or (kind == 2 and pq == 0)
         up_end, down_end = (4, 3) if long_up else (3, 4)
         if d < 0 and -d < up_end:
-            go(y_copy(pq, d, kind, 1))
+            y_copy(pq, d, kind, 1).start()
         if 0 < d < down_end:
-            go(y_copy(pq, d, kind, -1))
-        go(b_copy(pq, d, kind))
+            y_copy(pq, d, kind, -1).start()
+        b_copy(pq, d, kind).start()
 
     def enter(kind):
         q_copy(kind).wait_recv()
-        go(y_copy(1, 0, kind, 1))
-        go(y_copy(1, 0, kind, -1))
-        go(b_copy(1, 0, kind))
+        y_copy(1, 0, kind, 1).start()
+        y_copy(1, 0, kind, -1).start()
+        b_copy(1, 0, kind).start()
 
     def source_parts():
         both = 2 * PER
-        for pq in range(2):
-            for d in range(NY):
-                b_wait(pq, d, 2)
+        all_of(ga.at[:, :, 1 - c], b_ss.at[1], b_rs.at[2 * NY]).wait_recv()
         a = ga[...].reshape(2 * NY * 2 * both, part_k)
         t = [dot_t(a, w[:, k * part_k : (k + 1) * part_k]).reshape(4 * NY, both, 2 * vec) for k in range(2)]
         c_src[...] = (t[0][:, :PER] + t[1][:, PER:]).reshape(4 * NY * PER, 2 * vec)
 
     def fs_x(dx):
         xx = lax.rem(x + dx, NX)
-        return remote(fs.at[lax.rem(xx, 2), lax.div(xx, 2)], rfs.at[dx - 1], e_ss.at[0, dx], e_rs.at[0, dx], dev(dx=dx))
+        return remote(fs.at[lax.rem(xx, 2), lax.div(xx, 2)], rfs.at[dx - 1], e_ss.at[0], e_rs.at[0], dev(dx=dx))
 
     def fs_z(k):
-        return remote(fss.at[lax.rem(z + k, NZ)], rfsz.at[k], e_ss.at[1, k], e_rs.at[1, k], dev(dz=k))
+        return remote(fss.at[lax.rem(z + k, NZ)], rfsz.at[k], e_ss.at[1], e_rs.at[1], dev(dz=k))
 
     def fd_z(k):
-        return remote(fd.at[lax.rem(z + k, NZ)], rfd.at[k], e_ss.at[2, k], e_rs.at[2, k], dev(dz=k))
+        return remote(fd.at[lax.rem(z + k, NZ)], rfd.at[k], e_ss.at[2], e_rs.at[2], dev(dz=k))
 
     def fd_x(dx):
         xx = lax.rem(x + dx, NX)
-        return remote(fdd.at[lax.rem(xx, 2), lax.div(xx, 2)], rfdx.at[dx - 1], e_ss.at[3, dx], e_rs.at[3, dx], dev(dx=dx))
+        return remote(fdd.at[lax.rem(xx, 2), lax.div(xx, 2)], rfdx.at[dx - 1], e_ss.at[3], e_rs.at[3], dev(dx=dx))
 
     def source_send():
         sums = c_src[...]
@@ -278,7 +273,7 @@
                 for g in range(2):
                     fs[lax.rem(yb, 2), g, slot] = sums[r0 : r0 + both, g * vec : (g + 1) * vec]
         for dx in range(1, NX):
-            go(fs_x(dx))
+            fs_x(dx).start()
         block = jnp.floor((rel[:, 0:1] + 0.5) * (1.0 / (2 * PER)))
         at = rel[:, 0:1] - PER * block
         picked = pick_rows(jnp.where(at == iota((events, events), 1), 1.0, 0.0).astype(BF16), sums)
@@ -288,7 +283,7 @@
                 for g in range(2):
                     fd[zz, par, g] = picked[r0 : r0 + both, g * vec : (g + 1) * vec]
         for k in range(1, NZ):
-            go(fd_z(k))
+            fd_z(k).start()
 
     s_copy = remote(s_out, s_in, p_ss.at[4], p_rs.at[4], dev(dx=2))
 
@@ -317,21 +312,22 @@
             ).astype(BF16)
         g_out.start()
 
+    late = [rfs, rfsz.at[pl.ds(1, NZ - 1)], rfd.at[pl.ds(1, NZ - 1)], rfdx]
+
     def sources_on():
-        for dx in range(1, NX):
-            fs_x(dx).wait_recv()
+        all_of(late[0], e_ss.at[0], e_rs.at[0]).wait_recv()
         fss[...] = (fs[xl, h] + rfs[0]) + (rfs[1] + rfs[2])
         for k in range(1, NZ):
-            go(fs_z(k))
+            fs_z(k).start()
 
     def destinations_on():
+        all_of(late[2], e_ss.at[2], e_rs.at[2]).wait_recv()
         total = fd[z]
         for k in range(1, NZ):
-            fd_z(k).wait_recv()
             total = total + rfd[k]
         fdd[...] = total
         for dx in range(1, NX):
-            go(fd_x(dx))
+            fd_x(dx).start()
 
     def takes(*items):
         for item in items:
@@ -400,25 +396,31 @@
     o_from = jnp.where(hit_o > 0.5, two + (2 + in_core) * PER + t_less, o_from)
     order = jnp.where(o_from == iota((wide, wide), 1), 1.0, 0.0).astype(BF16)
     main, from_s, from_d = zs[z], fss[z], fdd[xl, h]
+    all_of(late[1], e_ss.at[1], e_rs.at[1]).wait_recv()
+    for k in range(1, NZ):
+        from_s = from_s + rfsz[k]
+    all_of(late[3], e_ss.at[3], e_rs.at[3]).wait_recv()
     for dx in range(1, NX):
-        fd_x(dx).wait_recv()
         from_d = from_d + rfdx[dx - 1]
+    others = pl.ds(1, NZ - 1)
+    all_of(rz.at[others], z_ss.at[0], z_rs.at[0]).wait_recv()
     for k in range(1, NZ):
-        fs_z(k).wait_recv()
-        from_s = from_s + rfsz[k]
-    for k in range(1, NZ):
-        remote(zs.at[0], rz.at[k], z_ss.at[k], z_rs.at[k], dev(dz=k)).wait_recv()
         main = main + rz[k]
     bias[...] = pick_rows(order, jnp.concatenate([main, from_s, from_d], axis=0))
 
     g_out.wait()
     for copy in started:
         copy.wait_send()
-    for dx in range(1, NX):
-        for slot in range(NZ):
-            remote(cs.at[0, 0, 0], rx.at[dx - 1, slot], x_ss.at[dx - 1, slot], x_rs.at[dx - 1, slot], dev(dx=dx)).wait_send()
-    for k in range(1, NZ):
-        remote(zs.at[0], rz.at[k], z_ss.at[k], z_rs.at[k], dev(dz=k)).wait_send()
+    around = pl.ds(1, NY - 1)
+    all_of(ga.at[:, around, c], y_ss.at[2], y_rs.at[0, 0, 0]).wait_send()
+    for k in range(2):
+        all_of(gb.at[:, around, k, c], y_ss.at[k], y_rs.at[0, 0, 0]).wait_send()
+    all_of(ga.at[:, :, c], b_ss.at[1], b_rs.at[0]).wait_send()
+    all_of(gb.at[:, :, :, c], b_ss.at[0], b_rs.at[0]).wait_send()
+    all_of(rx, x_ss.at[0], x_rs.at[0]).wait_send()
+    all_of(rz.at[others], z_ss.at[0], z_rs.at[0]).wait_send()
+    for n in range(4):
+        all_of(late[n], e_ss.at[n], e_rs.at[n]).wait_send()
 
 
 def local(cholesky, green_half, partners):
@@ -463,8 +465,8 @@
             pltpu.VMEM((256, 2 * vec), F32),
             pltpu.VMEM((256, 128), F32),
             dma((4,)),
-            dma((2, 3, 2, 4)), dma((2, NY, 3)), dma((2, NY, 3)), dma((2, NY, 3)), dma((5,)), dma((5,)),
-            dma((3, NZ)), dma((3, NZ)), dma((NZ,)), dma((NZ,)), dma((4, NZ)), dma((4, NZ)),
+            dma((3,)), dma((2, NY, 3)), dma((2,)), dma((2 * NY + 1,)), dma((5,)), dma((5,)),
+            dma((1,)), dma((NZ,)), dma((1,)), dma((1,)), dma((4,)), dma((4,)),
             pltpu.SemaphoreType.REGULAR((3,)),
         ],
         compiler_params=pltpu.CompilerParams(

time: 64.1 us -> 61.9 us (0.966)
  Pallas kernels: 60.9 us -> 58.7 us
    pallas_call x1, Pallas kernels: 60.9 us -> 58.7 us  [local(): pl.pallas_call(kernel, out_shape=(jax.ShapeDtypeStruct((rows, depth), BF1...]
where the time goes in v4:
time: 61.9 us; the launch traced here: 61.8 us
  Pallas kernels  58.7 us (95%)
  local copies, waits for them, and re-layouts  2.4 us (4%)
  between operations  0.65 us (1%)
    pallas_call x1, Pallas kernels, local(): pl.pallas_call(kernel, out_shape=(jax.ShapeDtypeStruct((rows, depth), BF1...  58.7 us
    unnamed x4, local copies, waits for them, and re-layouts  2.4 us

profile of v4, /device:TPU:24, one launch (start us, length us, event | category | flops | bytes accessed | tf_op | source)
XLA Modules:
  0.0 61.8 jit_solution(10148515717629121525)
XLA Ops:
  0.6 58.7 %shard_map.50 = (bf16[48,4096]{1,0:T(8,128)(2,1)}, f32[96,128]{1,0:T(8,128)}) custom-call(bf16[128,4096]{1,0:T(8,128)(2,1)} %chol.1, bf16[48,4096]{1,0:T(8,128)(2,1)} %green.1, s32[2,256]{1,0:T(2,128)} %bitcast.1), custom_call_target="tpu_custom_call" | custom-call | tf_op jit(solution)/shard_map/pallas_call | solution.py:434
  59.4 0.0 copy-start
  59.4 1.8 %copy.7 = bf16[48,4096]{1,0:T(8,128)(2,1)} copy(bf16[48,4096]{1,0:T(8,128)(2,1)} %get-tuple-element.4) | data formatting | bytes 786432
  61.1 0.0 copy-done
  61.1 0.6 %copy.8 = f32[96,128]{1,0:T(8,128)} copy(f32[96,128]{1,0:T(8,128)S(1)} %copy-done) | data formatting | bytes 98304
Async XLA Ops:
  59.4 1.8 %copy-start = (f32[96,128]{1,0:T(8,128)S(1)}, f32[96,128]{1,0:T(8,128)}, u32[]{:S(2)}) copy-start(f32[96,128]{1,0:T(8,128)} %get-tuple-element.5) | copy-start | bytes 147460
